TPU v7x, 32 devices: a whole 2x2x4 slice. The times are simulated.
32 devices in a mesh: sub: 8 (over z, y), grp: 4 (over x, core).
Axes of the slice: x: 2, y: 2, z: 4, core: 2. Of those that a mesh axis runs over, the one named last changes fastest.
Arguments:
- leaf_inverse: float32 [8, 4, 8, 256, 256], P('sub', 'grp'), may hold values from -0.375 to 0.375
- interior_rhs: float32 [8, 4, 8, 256, 128], P('sub', 'grp'), may hold values from -6 to 6
- interface_rhs: float32 [8, 4, 64, 128], P('sub', 'grp'), may hold values from -6 to 6
- project_basis: float32 [8, 4, 8, 4, 32, 256], P('sub', 'grp'), may hold values from -0.375 to 0.375
- lift_basis: float32 [8, 4, 8, 4, 32, 256], P('sub', 'grp'), may hold values from -0.5 to 0.5
- cluster_basis: float32 [8, 4, 32, 64], P('sub', 'grp'), may hold values from -0.1875 to 0.1875
- interface_inverse: float32 [4, 512, 512], P('grp'), may hold values from -0.25 to 0.25
- coarse_basis: float32 [4, 512, 128], P('grp'), may hold values from -0.25 to 0.25
- coarse_inverse: float32 [128, 128], replicated, may hold values from -0.25 to 0.25
- couplings: int32 [8, 4, 8, 4], P('sub', 'grp'), may hold values from 0 to 7, as said below
- ranks: int32 [8, 4, 8, 4], P('sub', 'grp'), may hold values from 8 to 32
- owners: int32 [4, 8], P('grp'), may hold values from 0 to 7, each once within a row
Outputs:
- interior: float32 [8, 4, 8, 256, 128], P('sub', 'grp')
- interface_solution: float32 [8, 4, 64, 128], P('sub', 'grp')
Inputs may be any that keep to these rules, and one draw needn't show every extreme that they name: `couplings`: entries name clusters of the same group. The 4 clusters of one leaf are distinct; among one subdomain's 8 leaves no cluster is named more than 4 times, and in each group one cluster is named exactly 4 times by every subdomain of the group. Each row is a permutation: owners[g, k] is the sub index holding cluster k of group g.
All inputs are finite; a program needn't handle non-finite values.
Results may differ from a plain program's by a relative error of at most 0.000071.
Values sent between devices are 32-bit elements; how exact they have to be, the bound alone decides.
A program may use at most 128 MiB of HBM per device.

v0:
```python
import jax
import jax.numpy as jnp
from jax import lax
from jax.sharding import PartitionSpec as P

highest = lax.Precision.HIGHEST


def shards(
    leaf_inverse,
    interior_rhs,
    interface_rhs,
    project_basis,
    lift_basis,
    cluster_basis,
    interface_inverse,
    coarse_basis,
    coarse_inverse,
    couplings,
    ranks,
    owners,
):
    linv_local = leaf_inverse[0, 0]
    leaves = couplings.shape[2]
    blocks = couplings.shape[3]
    rank_pad = project_basis.shape[4]
    port_count = interior_rhs.shape[4]
    cluster_width = cluster_basis.shape[3]
    sub_count = lax.axis_size("sub")
    block_count = leaves * blocks
    solved = jnp.einsum("lij,ljp->lip", linv_local, interior_rhs[0, 0], precision=highest)
    rank_mask = (
        jnp.arange(rank_pad, dtype=jnp.int32)[None, None, :] < ranks[0, 0][..., None]
    ).astype(jnp.float32)
    coefficients = (
        jnp.einsum("ljri,lip->ljrp", project_basis[0, 0], solved, precision=highest)
        * rank_mask[..., None]
    )
    flat_coef = coefficients.reshape(block_count, rank_pad, port_count)
    owner_table = owners[0]
    sub_range = jnp.arange(sub_count, dtype=jnp.int32)
    cluster_hot = (couplings[0, 0].reshape(block_count)[:, None] == sub_range[None, :]).astype(
        jnp.int32
    )
    target = jnp.sum(cluster_hot * owner_table[None, :], axis=1)
    owner_matrix = (owner_table[:, None] == sub_range[None, :]).astype(jnp.float32)
    capacity = max(2, block_count // sub_count)
    block_range = jnp.arange(block_count, dtype=jnp.int32)
    earlier = (target[:, None] == target[None, :]) & (block_range[None, :] < block_range[:, None])
    slot_index = jnp.sum(earlier.astype(jnp.int32), axis=1)
    slot_place = target * capacity + slot_index
    dispatch = (
        slot_place[:, None] == jnp.arange(sub_count * capacity, dtype=jnp.int32)[None, :]
    ).astype(jnp.float32)
    outgoing = jnp.einsum("mq,mrp->qrp", dispatch, flat_coef, precision=highest).reshape(
        sub_count, capacity, rank_pad, port_count
    )
    filled = jnp.sum(dispatch, axis=0).reshape(sub_count, capacity)
    incoming, filled_in = (
        lax.all_to_all(outgoing, "sub", split_axis=0, concat_axis=0, tiled=True),
        lax.all_to_all(filled, "sub", split_axis=0, concat_axis=0, tiled=True),
    )
    gathered_coef = jnp.sum(incoming, axis=(0, 1))
    own_basis = cluster_basis[0, 0]
    interface_terms = interface_rhs[0, 0] - lax.dot_general(
        own_basis, gathered_coef, (((0,), (0,)), ((), ())), precision=highest
    )
    port_share = port_count // sub_count
    by_share = interface_terms.T.reshape(sub_count, port_share * cluster_width)
    spread = lax.all_to_all(by_share, "sub", split_axis=0, concat_axis=0, tiled=True).reshape(
        sub_count, port_share, cluster_width
    )
    ordered = jnp.einsum("ks,spc->pkc", owner_matrix, spread, precision=highest).reshape(
        port_share, sub_count * cluster_width
    )
    local_part = lax.dot_general(
        ordered, interface_inverse[0], (((1,), (1,)), ((), ())), precision=highest
    )
    coarse_local = jnp.dot(ordered, coarse_basis[0], precision=highest)
    coarse_residual = lax.psum(coarse_local, "grp")
    coarse_solution = lax.dot_general(
        coarse_residual, coarse_inverse, (((1,), (1,)), ((), ())), precision=highest
    )
    solution = local_part + lax.dot_general(
        coarse_solution, coarse_basis[0], (((1,), (1,)), ((), ())), precision=highest
    )
    owner_order = jnp.einsum(
        "ks,pkc->spc",
        owner_matrix,
        solution.reshape(port_share, sub_count, cluster_width),
        precision=highest,
    )
    back_rows = lax.all_to_all(
        owner_order.reshape(sub_count, port_share * cluster_width),
        "sub",
        split_axis=0,
        concat_axis=0,
        tiled=True,
    )
    own_solution = back_rows.reshape(port_count, cluster_width).T
    lifted = jnp.dot(own_basis, own_solution, precision=highest)
    replies = filled_in[:, :, None, None] * lifted[None, None]
    returned = lax.all_to_all(replies, "sub", split_axis=0, concat_axis=0, tiled=True).reshape(
        -1, rank_pad, port_count
    )
    per_block = jnp.einsum("mq,qrp->mrp", dispatch, returned, precision=highest)
    per_block = per_block.reshape(leaves, blocks, rank_pad, port_count) * rank_mask[..., None]
    correction = jnp.einsum("ljri,ljrp->lip", lift_basis[0, 0], per_block, precision=highest)
    interior = solved - jnp.einsum("lij,ljp->lip", linv_local, correction, precision=highest)
    return (interior[None, None], own_solution[None, None])


def solution(mesh):
    in_specs = (
        P("sub", "grp", None, None, None),
        P("sub", "grp", None, None, None),
        P("sub", "grp", None, None),
        P("sub", "grp", None, None, None, None),
        P("sub", "grp", None, None, None, None),
        P("sub", "grp", None, None),
        P("grp", None, None),
        P("grp", None, None),
        P(),
        P("sub", "grp", None, None),
        P("sub", "grp", None, None),
        P("grp", None),
    )
    out_specs = (P("sub", "grp", None, None, None), P("sub", "grp", None, None))
    return jax.shard_map(shards, mesh=mesh, in_specs=in_specs, out_specs=out_specs, check_vma=False)
```

profile of v0, /device:TPU:0, one launch (start us, length us, event | category | flops | bytes accessed | tf_op | source)
XLA Modules:
  0.0 97.6 jit_solution(16663083689592707131)
XLA Ops:
  0.7 0.9 copy.63
  3.4 3.3 %fusion.2 = f32[8,256,128]{2,1,0:T(8,128)S(1)} fusion(f32[1,1,8,256,256]{4,3,2,1,0:T(8,128)S(1)} %copy-done, f32[1,1,8,256,128]{4,3,2,1,0:T(8,128)} %param.13), kind=kOutput, calls=%fused_computation.2 | convolution fusion | flops 805306368 | bytes 4194304 | tf_op jit(solution)/shard_map/lij,ljp->lip/dot_general | solution.py:31
  6.8 1.3 %convolution_multiply_fusion = f32[8,128,4,32]{1,3,2,0:T(8,128)S(1)} fusion(f32[8,256,128]{2,1,0:T(8,128)S(1)} %fusion.2, f32[1,1,8,4,32,256]{5,4,3,2,1,0:T(8,128)S(1)} %copy-done.1, f32[8,4,32]{2,1,0:T(4,128)S(1)} %fusion.34), kind=kOutput, calls=%fused_computation.8 | convolution fusion | flops 402784256 | bytes 2625536 | tf_op jit(solution)/shard_map/ljri,lip->ljrp/dot_general | solution.py:36
  8.0 0.8 fusion.21
  8.8 21.7 %all_to_all.38 = f32[8,4,32,128]{3,1,2,0:T(4,128)} all-to-all(f32[8,4,32,128]{3,1,2,0:T(4,128)S(1)} %fusion.21), channel_id=1, replica_groups=mesh['sub'=8,'grp'=4] {'sub'}, dimensions={0} | all-to-all | bytes 1048576 | tf_op jit(solution)/shard_map/all_to_all | solution.py:60
  30.5 1.1 %reduce_sum.39 = f32[32,128]{1,0:T(8,128)S(1)} reduce(f32[8,4,32,128]{3,1,2,0:T(4,128)} %all_to_all.38, f32[]{:T(128)} %constant.7.clone.1), dimensions={0,1}, to_apply=%region_3.0 | reduce | flops 126976 | bytes 540676 | tf_op jit(solution)/shard_map/reduce_sum | solution.py:63
  32.2 10.1 %all_to_all.39 = f32[8,1,1024]{2,1,0:T(1,128)S(1)} all-to-all(f32[8,1,1024]{2,1,0:T(1,128)S(1)} %all_to_all.32), channel_id=1, replica_groups=mesh['sub'=8,'grp'=4] {'sub'}, dimensions={0} | all-to-all | bytes 65536 | tf_op jit(solution)/shard_map/all_to_all | solution.py:70
  42.4 0.9 convolution_bitcast_fusion.1
  43.6 2.2 %fusion.17 = f32[16,512]{1,0:T(8,128)S(1)} fusion(f32[16,512]{1,0:T(8,128)S(1)} %reshape.103, f32[1,512,512]{2,1,0:T(8,128)} %param.18), kind=kOutput, calls=%fused_computation.19 | convolution fusion | flops 50331648 | bytes 1114112 | tf_op jit(solution)/shard_map/dot_general | solution.py:76
  45.8 5.8 %psum.7 = f32[16,128]{1,0:T(8,128)S(1)} all-reduce(f32[16,128]{1,0:T(8,128)S(1)} %fusion.26), channel_id=1, replica_groups=mesh['sub'=8,'grp'=4] {'grp'}, use_global_device_ids=true, to_apply=%region_4.0 | all-reduce | flops 2048 | bytes 16384 | tf_op jit(solution)/shard_map/psum | solution.py:80
  51.6 1.0 %fusion.44 = f32[16,128]{1,0:T(8,128)S(1)} fusion(f32[16,128]{1,0:T(8,128)S(1)} %psum.7, f32[128,128]{1,0:T(8,128)} %param.20), kind=kOutput, calls=%fused_computation.57 | convolution fusion | flops 3145728 | bytes 81920 | tf_op jit(solution)/shard_map/dot_general | solution.py:81
  53.1 0.9 convolution_bitcast_fusion.2
  54.7 3.3 %all-to-all-start.3 = ((f32[8,1,1024]{2,1,0:T(1,128)}), f32[8,1,1024]{2,1,0:T(1,128)S(1)}, u32[]{:S(2)}, u32[]{:S(2)}) async-start(f32[8,1,1024]{2,1,0:T(1,128)} %copy.74), calls=%async_computation.3 | async-start | bytes 65536 | tf_op jit(solution)/shard_map/all_to_all | solution.py:93
  58.0 0.8 convert_reduce_fusion
  59.5 5.2 %all-to-all-done.3 = f32[8,1,1024]{2,1,0:T(1,128)S(1)} async-done(((f32[8,1,1024]{2,1,0:T(1,128)}), f32[8,1,1024]{2,1,0:T(1,128)S(1)}, u32[]{:S(2)}, u32[]{:S(2)}) %all-to-all-start.3) | async-done | bytes 32800 | tf_op jit(solution)/shard_map/all_to_all | solution.py:93
  64.7 3.3 %all-to-all-start = ((f32[8,1,4]{2,1,0:T(1,128)}), f32[8,1,4]{2,1,0:T(1,128)S(1)}, u32[]{:S(2)}, u32[]{:S(2)}) async-start(f32[8,1,4]{2,1,0:T(1,128)} %bitcast.6), calls=%async_computation | async-start | bytes 8192 | tf_op jit(solution)/shard_map/all_to_all | solution.py:61
  68.2 0.9 convolution_bitcast_fusion.4
  69.1 5.2 %all-to-all-done = f32[8,1,4]{2,1,0:T(1,128)S(1)} async-done(((f32[8,1,4]{2,1,0:T(1,128)}), f32[8,1,4]{2,1,0:T(1,128)S(1)}, u32[]{:S(2)}, u32[]{:S(2)}) %all-to-all-start) | async-done | bytes 160 | tf_op jit(solution)/shard_map/all_to_all | solution.py:61
  74.3 0.9 broadcast_multiply_fusion
  75.2 4.1 %all-to-all-start.4 = ((f32[8,4,32,128]{3,1,2,0:T(4,128)}), f32[8,4,32,128]{3,1,2,0:T(4,128)}, u32[]{:S(2)}, u32[]{:S(2)}) async-start(f32[8,4,32,128]{3,1,2,0:T(4,128)} %broadcast_multiply_fusion), calls=%async_computation.4 | async-start | bytes 1048576 | tf_op jit(solution)/shard_map/all_to_all | solution.py:103
  80.4 11.5 %all-to-all-done.4 = f32[8,4,32,128]{3,1,2,0:T(4,128)} async-done(((f32[8,4,32,128]{3,1,2,0:T(4,128)}), f32[8,4,32,128]{3,1,2,0:T(4,128)}, u32[]{:S(2)}, u32[]{:S(2)}) %all-to-all-start.4) | async-done | bytes 524320 | tf_op jit(solution)/shard_map/all_to_all | solution.py:103
  91.9 1.3 %copy.75 = f32[8,4,32,128]{3,1,0,2:T(4,128)S(1)} copy(f32[8,4,32,128]{3,1,2,0:T(4,128)} %all-to-all-done.4) | data formatting | bytes 1048576 | tf_op jit(solution)/shard_map/all_to_all | solution.py:103
  93.6 1.1 %convolution_bitcast_fusion = f32[8,128,256]{2,1,0:T(8,128)S(1)} fusion(f32[1,1,8,4,32,256]{5,4,3,2,1,0:T(8,128)S(1)} %copy-done.2, f32[8,4,32,128]{3,0,2,1:T(8,128)S(1)} %convolution_multiply_fusion.1), kind=kOutput, calls=%fused_computation.7 | convolution fusion | flops 402653184 | bytes 2621440 | tf_op jit(solution)/shard_map/ljri,ljrp->lip/dot_general | solution.py:108
  94.7 2.9 %fusion.10 = f32[1,1,8,256,128]{4,3,2,1,0:T(8,128)} fusion(f32[8,256,128]{2,1,0:T(8,128)S(1)} %fusion.2, f32[8,128,256]{2,1,0:T(8,128)S(1)} %convolution_bitcast_fusion, f32[1,1,8,256,256]{4,3,2,1,0:T(8,128)S(1)} %copy-done), kind=kOutput, calls=%fused_computation.6 | convolution fusion | flops 805568512 | bytes 5242880 | tf_op jit(solution)/shard_map/lij,ljp->lip/dot_general | solution.py:109
  (43 shorter events, 6.2 us)
Async XLA Ops:
  0.6 2.8 %copy-start = (f32[1,1,8,256,256]{4,3,2,1,0:T(8,128)S(1)}, f32[1,1,8,256,256]{4,3,2,1,0:T(8,128)}, u32[]{:S(2)}) copy-start(f32[1,1,8,256,256]{4,3,2,1,0:T(8,128)} %param.12) | copy-start | bytes 6291460
  2.6 5.5 %copy-start.6 = (s32[32]{0:T(128)}, s32[32]{0:T(128)S(1)}, u32[]{:S(2)}) copy-start(s32[32]{0:T(128)S(1)} %multiply_add_fusion.1) | copy-start | bytes 388
  3.4 3.3 %copy-start.1 = (f32[1,1,8,4,32,256]{5,4,3,2,1,0:T(8,128)S(1)}, f32[1,1,8,4,32,256]{5,4,3,2,1,0:T(8,128)}, u32[]{:S(2)}) copy-start(f32[1,1,8,4,32,256]{5,4,3,2,1,0:T(8,128)} %param.15) | copy-start | bytes 3145732
  6.7 25.0 %copy-start.4 = (f32[1,1,32,64]{3,2,1,0:T(8,128)S(1)}, f32[1,1,32,64]{3,2,1,0:T(8,128)}, u32[]{:S(2)}) copy-start(f32[1,1,32,64]{3,2,1,0:T(8,128)} %param.17) | copy-start | bytes 24580
  6.7 25.0 %copy-start.5 = (f32[1,1,64,128]{3,2,1,0:T(8,128)S(1)}, f32[1,1,64,128]{3,2,1,0:T(8,128)}, u32[]{:S(2)}) copy-start(f32[1,1,64,128]{3,2,1,0:T(8,128)} %param.14) | copy-start | bytes 98308
  8.0 35.3 %copy-start.3 = (f32[1,512,128]{2,1,0:T(8,128)S(1)}, f32[1,512,128]{2,1,0:T(8,128)}, u32[]{:S(2)}) copy-start(f32[1,512,128]{2,1,0:T(8,128)} %param.19) | copy-start | bytes 786436
  43.4 36.1 %copy-start.7 = (s32[32]{0:T(128)S(1)}, s32[32]{0:T(128)}, u32[]{:S(2)}) copy-start(s32[32]{0:T(128)} %copy-done.6) | copy-start | bytes 388
  54.7 10.0 %all-to-all-start.3 = ((f32[8,1,1024]{2,1,0:T(1,128)}), f32[8,1,1024]{2,1,0:T(1,128)S(1)}, u32[]{:S(2)}, u32[]{:S(2)}) async-start(f32[8,1,1024]{2,1,0:T(1,128)} %copy.74), calls=%async_computation.3 | async-start | bytes 65536 | tf_op jit(solution)/shard_map/all_to_all | solution.py:93
  64.7 9.6 %all-to-all-start = ((f32[8,1,4]{2,1,0:T(1,128)}), f32[8,1,4]{2,1,0:T(1,128)S(1)}, u32[]{:S(2)}, u32[]{:S(2)}) async-start(f32[8,1,4]{2,1,0:T(1,128)} %bitcast.6), calls=%async_computation | async-start | bytes 8192 | tf_op jit(solution)/shard_map/all_to_all | solution.py:61
  75.2 16.7 %all-to-all-start.4 = ((f32[8,4,32,128]{3,1,2,0:T(4,128)}), f32[8,4,32,128]{3,1,2,0:T(4,128)}, u32[]{:S(2)}, u32[]{:S(2)}) async-start(f32[8,4,32,128]{3,1,2,0:T(4,128)} %broadcast_multiply_fusion), calls=%async_computation.4 | async-start | bytes 1048576 | tf_op jit(solution)/shard_map/all_to_all | solution.py:103
  91.9 1.7 %copy-start.2 = (f32[1,1,8,4,32,256]{5,4,3,2,1,0:T(8,128)S(1)}, f32[1,1,8,4,32,256]{5,4,3,2,1,0:T(8,128)}, u32[]{:S(2)}) copy-start(f32[1,1,8,4,32,256]{5,4,3,2,1,0:T(8,128)} %param.16) | copy-start | bytes 3145732
where the time goes:
time: 98.3 us; the launch traced here: 97.6 us
  blocking collectives  37.6 us (38%)
  waiting for transfers between devices  22 us (22%)
  matrix products  16.5 us (17%)
  starting transfers between devices  10.8 us (11%)
  local copies, waits for them, and re-layouts  5.94 us (6%)
  other arithmetic  4.01 us (4%)
    all_to_all x1, blocking collectives, shards(): lax.all_to_all(outgoing, 'sub', split_axis=0, concat_axis=0, tiled=True)  21.7 us
    all_to_all x1, waiting for transfers between devices, shards(): lax.all_to_all(replies, 'sub', split_axis=0, concat_axis=0, tiled=True)  11.5 us
    all_to_all x1, blocking collectives, shards(): lax.all_to_all(by_share, 'sub', split_axis=0, concat_axis=0, tiled=True)  10.1 us
    psum x1, blocking collectives, shards(): coarse_residual = lax.psum(coarse_local, 'grp')  5.77 us
    all_to_all x1, waiting for transfers between devices, shards(): lax.all_to_all(filled, 'sub', split_axis=0, concat_axis=0, tiled=True)  5.25 us
    all_to_all x1, waiting for transfers between devices, shards(): lax.all_to_all(owner_order.reshape(sub_count, port_share * cluster_width)...  5.17 us
    all_to_all x1, starting transfers between devices, shards(): lax.all_to_all(replies, 'sub', split_axis=0, concat_axis=0, tiled=True)  4.14 us
    all_to_all x1, starting transfers between devices, shards(): lax.all_to_all(owner_order.reshape(sub_count, port_share * cluster_width)...  3.34 us
  transfers between devices with their start and end apart: 3, of which 3 were waited for; matrix products, arithmetic and copies ran while one was open for 3% of the time, Pallas kernels for 0%

commit v1 on v0

--- a/solution.py
+++ b/solution.py
@@ -1,9 +1,379 @@
+import functools
+
 import jax
 import jax.numpy as jnp
 from jax import lax
+from jax.experimental import pallas as pl
+from jax.experimental.pallas import tpu as pltpu
 from jax.sharding import PartitionSpec as P
 
 highest = lax.Precision.HIGHEST
+MESH = pl.DeviceIdType.MESH
+F32 = jnp.float32
+BF16 = jnp.bfloat16
+
+
+def split(x):
+    high = x.astype(BF16)
+    return high, (x - high.astype(F32)).astype(BF16)
+
+
+def dot(a, b, dims=((1,), (0,))):
+    return lax.dot_general(a, b, (dims, ((), ())), preferred_element_type=F32)
+
+
+def product(a, b, dims=((1,), (0,))):
+    return dot(a[0], b[0], dims) + dot(a[0], b[1], dims) + dot(a[1], b[0], dims)
+
+
+def narrow(a, b):
+    width = b[0].shape[1]
+    both = dot(a[0], jnp.concatenate([b[0], b[1]], axis=1))
+    return both[:, :width] + both[:, width:] + dot(a[1], b[0])
+
+
+def kernel(
+    n,
+    groups,
+    linv_hbm,
+    rhs_hbm,
+    irhs_hbm,
+    proj_hbm,
+    lift_hbm,
+    basis_hbm,
+    inverse_hbm,
+    coarse_hbm,
+    cinv_hbm,
+    couplings,
+    ranks,
+    owners,
+    interior_hbm,
+    own_out,
+    linv,
+    rhs,
+    proj,
+    lift,
+    inverse,
+    coarse,
+    cinv,
+    g_basis,
+    g_irhs,
+    sums,
+    coarse_out,
+    in_sums,
+    in_coarse,
+    mid,
+    in_mid,
+    g_sums,
+    g_coarse,
+    bct,
+    gain,
+    base,
+    solved,
+    back,
+    lifted,
+    result,
+    leaf_sem,
+    misc_sem,
+    out_sem,
+    pre_send,
+    pre_recv,
+    a_send,
+    a_recv,
+    m_send,
+    m_recv,
+    b_send,
+    b_recv,
+):
+    leaves, ls, ports = rhs.shape
+    blocks = couplings.shape[1]
+    rank = g_basis.shape[1]
+    cs = g_basis.shape[2]
+    nco = coarse.shape[2]
+    piece = nco // n
+    me = lax.axis_index("sub")
+    my_group = lax.axis_index("grp")
+
+    def leaf_copy(l, which):
+        pair = ((linv_hbm, linv), (rhs_hbm, rhs), (proj_hbm, proj), (lift_hbm, lift))[which]
+        return pltpu.make_async_copy(pair[0].at[l], pair[1].at[l], leaf_sem.at[which, l])
+
+    barrier = pltpu.get_barrier_semaphore()
+    for d in range(1, n):
+        pl.semaphore_signal(barrier, inc=1, device_id=(lax.rem(me + d, n), my_group), device_id_type=MESH)
+    for d in range(1, groups):
+        pl.semaphore_signal(barrier, inc=1, device_id=(me, lax.rem(my_group + d, groups)), device_id_type=MESH)
+    for l in range(leaves):
+        for which in range(3):
+            leaf_copy(l, which).start()
+    misc = (
+        pltpu.make_async_copy(basis_hbm, g_basis.at[me], misc_sem.at[0]),
+        pltpu.make_async_copy(irhs_hbm, g_irhs.at[me], misc_sem.at[1]),
+        pltpu.make_async_copy(coarse_hbm, coarse, misc_sem.at[2]),
+        pltpu.make_async_copy(inverse_hbm, inverse, misc_sem.at[3]),
+        pltpu.make_async_copy(cinv_hbm, cinv, misc_sem.at[4]),
+    )
+    for copy in misc:
+        copy.start()
+    for l in range(leaves):
+        leaf_copy(l, 3).start()
+
+    sums[...] = jnp.zeros_like(sums)
+    row_of = lax.broadcasted_iota(jnp.int32, (rank, ports), 0)
+
+    def leaf_forward(l):
+        for which in range(3):
+            leaf_copy(l, which).wait()
+        both = product(split(proj[l]), split(linv[l]))
+        coef = narrow(split(both), split(rhs[l]))
+        for j in range(blocks):
+            kept = jnp.where(row_of < ranks[l, j], coef[j * rank : (j + 1) * rank], 0.0)
+            for k in range(n):
+                sums[k] += jnp.where(couplings[l, j] == k, kept, 0.0)
+
+    leaf_forward(0)
+
+    pl.semaphore_wait(barrier, n - 1 + groups - 1)
+
+    def peer(d):
+        return (lax.rem(me + d, n), my_group)
+
+    def source(d):
+        return lax.rem(me - d + n, n)
+
+    def pre_copy(d, which, slot):
+        src, dst = ((basis_hbm, g_basis), (irhs_hbm, g_irhs))[which]
+        return pltpu.make_async_remote_copy(
+            src_ref=src, dst_ref=dst.at[slot], send_sem=pre_send.at[which, d], recv_sem=pre_recv.at[which, d],
+            device_id=peer(d), device_id_type=MESH,
+        )
+
+    for which in range(2):
+        for d in range(1, n):
+            pre_copy(d, which, me).start()
+
+    pl.loop(1, leaves)(leaf_forward)
+
+    def sums_copy(d):
+        return pltpu.make_async_remote_copy(
+            src_ref=sums.at[lax.rem(me + d, n)], dst_ref=in_sums.at[d], send_sem=a_send.at[0, d],
+            recv_sem=a_recv.at[0, d], device_id=peer(d), device_id_type=MESH,
+        )
+
+    def coarse_copy(d):
+        return pltpu.make_async_remote_copy(
+            src_ref=coarse_out.at[lax.rem(me + d, n)], dst_ref=in_coarse.at[d], send_sem=a_send.at[1, d],
+            recv_sem=a_recv.at[1, d], device_id=peer(d), device_id_type=MESH,
+        )
+
+    for d in range(1, n):
+        sums_copy(d).start()
+
+    for copy in misc:
+        copy.wait()
+    for which in range(2):
+        for d in range(1, n):
+            pre_copy(d, which, source(d)).wait_recv()
+
+    stacked = jnp.concatenate([g_basis[owners[0, k]] for k in range(n)], axis=0)
+    wide = jnp.concatenate([stacked] * n, axis=1)
+    diag_row = lax.broadcasted_iota(jnp.int32, wide.shape, 0) // rank
+    diag_col = lax.broadcasted_iota(jnp.int32, wide.shape, 1) // cs
+    diagonal = split(jnp.where(diag_row == diag_col, wide, 0.0))
+    own = jnp.int32(0)
+    for k in range(n):
+        own = jnp.where(owners[0, k] == me, k, own)
+    coarse_pair = split(coarse[...].reshape(n * cs, nco))
+    basis_coarse = narrow(diagonal, coarse_pair)
+    own_coarse = coarse[own]
+    bct[...] = basis_coarse.T
+    sums_pair = split(sums[...].reshape(n * rank, ports))
+    part = narrow(split(own_coarse.T), split(g_irhs[me])) - narrow(split(bct[...]), sums_pair)
+    coarse_out[...] = part.reshape(n, piece, ports)
+    for d in range(1, n):
+        coarse_copy(d).start()
+
+    own_rows = inverse[own]
+    inverse_pair = split(inverse[...].reshape(n * cs, n * cs))
+    left = jnp.concatenate([product(diagonal, inverse_pair), own_rows], axis=0)
+    left_pair = split(left)
+    irhs_all = jnp.concatenate([g_irhs[owners[0, k]] for k in range(n)], axis=0)
+    base[...] = narrow(left_pair, split(irhs_all))
+    gain[:, : n * rank] = -product(left_pair, diagonal, ((1,), (1,)))
+    coarse_left = jnp.concatenate([basis_coarse, own_coarse], axis=0)
+    gain[:, n * rank :] = narrow(split(coarse_left), split(cinv[...]))
+
+    def gather_copy(d, which, slot):
+        ref = (g_sums, g_coarse)[which]
+        return pltpu.make_async_remote_copy(
+            src_ref=ref.at[me], dst_ref=ref.at[slot], send_sem=b_send.at[which, d], recv_sem=b_recv.at[which, d],
+            device_id=peer(d), device_id_type=MESH,
+        )
+
+    total = sums[me]
+    for d in range(1, n):
+        sums_copy(d).wait_recv()
+        total = total + in_sums[d]
+    g_sums[me] = total
+    for d in range(1, n):
+        gather_copy(d, 0, me).start()
+
+    def mid_copy(d):
+        return pltpu.make_async_remote_copy(
+            src_ref=mid, dst_ref=in_mid.at[d], send_sem=m_send.at[d], recv_sem=m_recv.at[d],
+            device_id=(me, lax.rem(my_group + d, groups)), device_id_type=MESH,
+        )
+
+    coarse_total = coarse_out[me]
+    for d in range(1, n):
+        coarse_copy(d).wait_recv()
+        coarse_total = coarse_total + in_coarse[d]
+    mid[...] = coarse_total
+    for d in range(1, groups):
+        mid_copy(d).start()
+
+    def leaf_middle(l):
+        leaf_copy(l, 3).wait()
+        inv = split(linv[l])
+        solved[l] = narrow(inv, split(rhs[l]))
+        spread = product(inv, split(lift[l]), ((1,), (1,)))
+        back[l] = jnp.concatenate(split(spread), axis=1)
+
+    half = leaves // 4
+    pl.loop(0, half)(leaf_middle)
+
+    for d in range(1, groups):
+        mid_copy(d).wait_recv()
+        coarse_total = coarse_total + in_mid[d]
+    g_coarse[me] = coarse_total
+    for d in range(1, n):
+        gather_copy(d, 1, me).start()
+
+    pl.loop(half, leaves)(leaf_middle)
+
+    for which in range(2):
+        for d in range(1, n):
+            gather_copy(d, which, source(d)).wait_recv()
+
+    known = jnp.concatenate([g_sums[...].reshape(n * rank, ports), g_coarse[...].reshape(nco, ports)], axis=0)
+    final = base[...] + narrow(split(gain[...]), split(known))
+    lifted[...] = final[: n * rank].reshape(n, rank, ports)
+    own_out[...] = final[n * rank :]
+
+    def out_copy(l):
+        return pltpu.make_async_copy(result.at[l], interior_hbm.at[l], out_sem.at[l])
+
+    @pl.loop(0, leaves)
+    def leaf_back(l):
+        rows = []
+        for j in range(blocks):
+            rows.append(jnp.where(row_of < ranks[l, j], lifted[couplings[l, j]], 0.0))
+        pair = jnp.concatenate(split(jnp.concatenate(rows, axis=0)), axis=1)
+        both = dot(back[l], jnp.concatenate([pair, pair], axis=0))
+        result[l] = solved[l] - (both[:, :ports] + both[:, ports:])
+        out_copy(l).start()
+
+    for l in range(leaves):
+        out_copy(l).wait()
+    for d in range(1, n):
+        for which in range(2):
+            pre_copy(d, which, me).wait_send()
+            gather_copy(d, which, me).wait_send()
+        sums_copy(d).wait_send()
+        coarse_copy(d).wait_send()
+    for d in range(1, groups):
+        mid_copy(d).wait_send()
+
+
+def fused(
+    leaf_inverse,
+    interior_rhs,
+    interface_rhs,
+    project_basis,
+    lift_basis,
+    cluster_basis,
+    interface_inverse,
+    coarse_basis,
+    coarse_inverse,
+    couplings,
+    ranks,
+    owners,
+):
+    n = lax.axis_size("sub")
+    groups = lax.axis_size("grp")
+    leaves, ls = leaf_inverse.shape[2:4]
+    ports = interior_rhs.shape[4]
+    blocks, rank = project_basis.shape[3:5]
+    cs = cluster_basis.shape[3]
+    nig = interface_inverse.shape[1]
+    nco = coarse_basis.shape[2]
+    piece = nco // n
+    hbm = pl.BlockSpec(memory_space=pl.ANY)
+    smem = pl.BlockSpec(memory_space=pltpu.SMEM)
+    dma = pltpu.SemaphoreType.DMA
+    interior, own = pl.pallas_call(
+        functools.partial(kernel, n, groups),
+        out_shape=(
+            jax.ShapeDtypeStruct((leaves, ls, ports), F32),
+            jax.ShapeDtypeStruct((cs, ports), F32),
+        ),
+        in_specs=[hbm] * 9 + [smem] * 3,
+        out_specs=(hbm, pl.BlockSpec(memory_space=pltpu.VMEM)),
+        scratch_shapes=[
+            pltpu.VMEM((leaves, ls, ls), F32),
+            pltpu.VMEM((leaves, ls, ports), F32),
+            pltpu.VMEM((leaves, blocks * rank, ls), F32),
+            pltpu.VMEM((leaves, blocks * rank, ls), F32),
+            pltpu.VMEM((n, cs, nig), F32),
+            pltpu.VMEM((n, cs, nco), F32),
+            pltpu.VMEM((nco, nco), F32),
+            pltpu.VMEM((n, rank, cs), F32),
+            pltpu.VMEM((n, cs, ports), F32),
+            pltpu.VMEM((n, rank, ports), F32),
+            pltpu.VMEM((n, piece, ports), F32),
+            pltpu.VMEM((n, rank, ports), F32),
+            pltpu.VMEM((n, piece, ports), F32),
+            pltpu.VMEM((piece, ports), F32),
+            pltpu.VMEM((groups, piece, ports), F32),
+            pltpu.VMEM((n, rank, ports), F32),
+            pltpu.VMEM((n, piece, ports), F32),
+            pltpu.VMEM((nco, n * rank), F32),
+            pltpu.VMEM((n * rank + cs, n * rank + nco), F32),
+            pltpu.VMEM((n * rank + cs, ports), F32),
+            pltpu.VMEM((leaves, ls, ports), F32),
+            pltpu.VMEM((leaves, ls, 2 * blocks * rank), BF16),
+            pltpu.VMEM((n, rank, ports), F32),
+            pltpu.VMEM((leaves, ls, ports), F32),
+            dma((4, leaves)),
+            dma((5,)),
+            dma((leaves,)),
+            dma((2, n)),
+            dma((2, n)),
+            dma((2, n)),
+            dma((2, n)),
+            dma((groups,)),
+            dma((groups,)),
+            dma((2, n)),
+            dma((2, n)),
+        ],
+        compiler_params=pltpu.CompilerParams(
+            collective_id=0, has_side_effects=True, vmem_limit_bytes=48 * 1024 * 1024
+        ),
+    )(
+        leaf_inverse[0, 0],
+        interior_rhs[0, 0],
+        interface_rhs[0, 0],
+        project_basis.reshape(leaves, blocks * rank, ls),
+        lift_basis.reshape(leaves, blocks * rank, ls),
+        cluster_basis[0, 0],
+        interface_inverse.reshape(n, cs, nig),
+        coarse_basis.reshape(n, cs, nco),
+        coarse_inverse,
+        couplings[0, 0],
+        ranks[0, 0],
+        owners,
+    )
+    return interior[None, None], own[None, None]
 
 
 def shards(
@@ -126,4 +496,5 @@
         P("grp", None),
     )
     out_specs = (P("sub", "grp", None, None, None), P("sub", "grp", None, None))
-    return jax.shard_map(shards, mesh=mesh, in_specs=in_specs, out_specs=out_specs, check_vma=False)
+    body = fused if mesh.shape["sub"] <= 8 else shards
+    return jax.shard_map(body, mesh=mesh, in_specs=in_specs, out_specs=out_specs, check_vma=False)

time: 98.3 us -> 50.6 us (0.51)
  blocking collectives: 37.6 us -> 0 us
  Pallas kernels: 0 us -> 37.5 us
  waiting for transfers between devices: 22 us -> 0 us
  matrix products: 16.5 us -> 0 us
  starting transfers between devices: 10.8 us -> 0 us
  local copies, waits for them, and re-layouts: 5.94 us -> 11.9 us
  other arithmetic: 4.01 us -> 0 us
    pallas_call x0 -> x1, Pallas kernels: none -> 37.5 us  [fused(): pl.pallas_call(functools.partial(kernel, n, groups), out_shape=(jax.Shape...]
    all_to_all x2 -> x0, blocking collectives: 31.8 us -> none  [the longest x1 21.7 us: shards(): lax.all_to_all(outgoing, 'sub', split_axis=0, concat_axis=0, tiled=True)]
    all_to_all x3 -> x0, waiting for transfers between devices: 22 us -> none  [the longest x1 11.5 us: shards(): lax.all_to_all(replies, 'sub', split_axis=0, concat_axis=0, tiled=True)]
    dot_general x14 -> x0, matrix products: 16.5 us -> none  [the longest x1 3.27 us: shards(): jnp.einsum('lij,ljp->lip', linv_local, interior_rhs[0, 0], precision=high...]
    all_to_all x3 -> x0, starting transfers between devices: 10.8 us -> none  [the longest x1 4.14 us: shards(): lax.all_to_all(replies, 'sub', split_axis=0, concat_axis=0, tiled=True)]
    unnamed x18 -> x20, local copies, waits for them, and re-layouts: 1.66 us -> 10.4 us
    psum x1 -> x0, blocking collectives: 5.77 us -> none  [shards(): coarse_residual = lax.psum(coarse_local, 'grp')]
    reduce_sum x4 -> x0, other arithmetic: 2.84 us -> none  [the longest x1 1.14 us: shards(): gathered_coef = jnp.sum(incoming, axis=(0, 1))]
  transfers between devices with their start and end apart: 3 -> 0, of which waited for: 3 -> 0; matrix products, arithmetic and copies ran while one was open for 3% -> 0% of each run, Pallas kernels for 0% -> 0%
where the time goes in v1:
time: 50.6 us; the launch traced here: 50 us
  Pallas kernels  37.5 us (74%)
  local copies, waits for them, and re-layouts  11.9 us (24%)
  between operations  0.65 us (1%)
    pallas_call x1, Pallas kernels, fused(): pl.pallas_call(functools.partial(kernel, n, groups), out_shape=(jax.Shape...  37.5 us
    unnamed x20, local copies, waits for them, and re-layouts  10.4 us

profile of v1, /device:TPU:0, one launch (start us, length us, event | category | flops | bytes accessed | tf_op | source)
XLA Modules:
  0.0 50.0 jit_solution(1585919628082358684)
XLA Ops:
  0.6 0.8 %copy.14.couplings = s32[8,4]{1,0:T(8,128)S(1)} copy(s32[8,4]{0,1:T(4,128)} %bitcast.22) | data formatting | bytes 256 | tf_op jit(solution)/shard_map/squeeze | solution.py:372
  1.4 0.8 %copy.15.ranks = s32[8,4]{1,0:T(8,128)S(1)} copy(s32[8,4]{0,1:T(4,128)} %bitcast.23) | data formatting | bytes 256 | tf_op jit(solution)/shard_map/squeeze | solution.py:373
  2.1 0.0 copy-start
  2.1 1.2 %copy-done = f32[1,1,8,256,128]{4,3,2,1,0:T(8,128)S(1)} copy-done((f32[1,1,8,256,128]{4,3,2,1,0:T(8,128)S(1)}, f32[1,1,8,256,128]{4,3,2,1,0:T(8,128)}, u32[]{:S(2)}) %copy-start) | copy-done | bytes 1048600
  3.4 0.0 copy-start.1
  3.4 1.2 %copy-done.1 = f32[1,1,8,4,32,256]{5,4,3,2,1,0:T(8,128)S(1)} copy-done((f32[1,1,8,4,32,256]{5,4,3,2,1,0:T(8,128)S(1)}, f32[1,1,8,4,32,256]{5,4,3,2,1,0:T(8,128)}, u32[]{:S(2)}) %copy-start.1) | copy-done | bytes 1048600
  4.6 0.0 copy-start.2
  4.6 1.2 %copy-done.2 = f32[1,1,8,4,32,256]{5,4,3,2,1,0:T(8,128)S(1)} copy-done((f32[1,1,8,4,32,256]{5,4,3,2,1,0:T(8,128)S(1)}, f32[1,1,8,4,32,256]{5,4,3,2,1,0:T(8,128)}, u32[]{:S(2)}) %copy-start.2) | copy-done | bytes 1048600
  5.8 0.0 copy-start.3
  5.8 1.2 %copy-done.3 = f32[1,512,512]{2,1,0:T(8,128)S(1)} copy-done((f32[1,512,512]{2,1,0:T(8,128)S(1)}, f32[1,512,512]{2,1,0:T(8,128)}, u32[]{:S(2)}) %copy-start.3) | copy-done | bytes 1048600
  7.0 0.0 copy-start.4
  7.0 0.9 %copy-done.4 = f32[1,512,128]{2,1,0:T(8,128)S(1)} copy-done((f32[1,512,128]{2,1,0:T(8,128)S(1)}, f32[1,512,128]{2,1,0:T(8,128)}, u32[]{:S(2)}) %copy-start.4) | copy-done | bytes 262168
  8.0 0.0 copy-start.5
  8.0 0.8 %copy-done.5 = f32[128,128]{1,0:T(8,128)S(1)} copy-done((f32[128,128]{1,0:T(8,128)S(1)}, f32[128,128]{1,0:T(8,128)}, u32[]{:S(2)}) %copy-start.5) | copy-done | bytes 65560
  8.8 0.0 copy-start.6
  8.8 0.8 %copy-done.6 = f32[1,1,64,128]{3,2,1,0:T(8,128)S(1)} copy-done((f32[1,1,64,128]{3,2,1,0:T(8,128)S(1)}, f32[1,1,64,128]{3,2,1,0:T(8,128)}, u32[]{:S(2)}) %copy-start.6) | copy-done | bytes 32792
  9.6 0.0 copy-start.7
  9.6 0.7 %copy-done.7 = f32[1,1,32,64]{3,2,1,0:T(8,128)S(1)} copy-done((f32[1,1,32,64]{3,2,1,0:T(8,128)S(1)}, f32[1,1,32,64]{3,2,1,0:T(8,128)}, u32[]{:S(2)}) %copy-start.7) | copy-done | bytes 8216
  10.3 0.0 copy-start.8
  10.3 0.7 %copy-done.8 = s32[1,8]{1,0:T(1,128)S(1)} copy-done((s32[1,8]{1,0:T(1,128)S(1)}, s32[1,8]{1,0:T(1,128)}, u32[]{:S(2)}) %copy-start.8) | copy-done | bytes 56
  11.0 37.5 %shard_map.131 = (f32[8,256,128]{2,1,0:T(8,128)S(1)}, f32[64,128]{1,0:T(8,128)S(1)}) custom-call(f32[8,256,256]{2,1,0:T(8,128)} %bitcast.21, f32[8,256,128]{2,1,0:T(8,128)S(1)} %bitcast.13, f32[64,128]{1,0:T(8,128)S(1)} %bitcast.18, f32[8,128,256]{2,1,0:T(8,128)S(1)} %bitcast.14, f32[8,128,256]{2,1,0:T(8,128)S(1)} %bitcast.15, f32[32,64]{1,0:T(8,128)S(1)} %bitcast.20, ...), custom_call_target="tpu_custom_call" | custom-call | tf_op jit(solution)/shard_map/pallas_call | solution.py:314
  48.4 1.0 %copy.18 = f32[1,1,8,256,128]{4,3,2,1,0:T(8,128)} copy(f32[1,1,8,256,128]{4,3,2,1,0:T(8,128)S(1)} %bitcast.12) | data formatting | bytes 2097152
  49.4 0.6 %copy.19 = f32[1,1,64,128]{3,2,1,0:T(8,128)} copy(f32[1,1,64,128]{3,2,1,0:T(8,128)S(1)} %bitcast.19) | data formatting | bytes 65536
Async XLA Ops:
  2.1 1.2 %copy-start = (f32[1,1,8,256,128]{4,3,2,1,0:T(8,128)S(1)}, f32[1,1,8,256,128]{4,3,2,1,0:T(8,128)}, u32[]{:S(2)}) copy-start(f32[1,1,8,256,128]{4,3,2,1,0:T(8,128)} %param.13) | copy-start | bytes 3145732
  3.4 1.2 %copy-start.1 = (f32[1,1,8,4,32,256]{5,4,3,2,1,0:T(8,128)S(1)}, f32[1,1,8,4,32,256]{5,4,3,2,1,0:T(8,128)}, u32[]{:S(2)}) copy-start(f32[1,1,8,4,32,256]{5,4,3,2,1,0:T(8,128)} %param.15) | copy-start | bytes 3145732
  4.6 1.2 %copy-start.2 = (f32[1,1,8,4,32,256]{5,4,3,2,1,0:T(8,128)S(1)}, f32[1,1,8,4,32,256]{5,4,3,2,1,0:T(8,128)}, u32[]{:S(2)}) copy-start(f32[1,1,8,4,32,256]{5,4,3,2,1,0:T(8,128)} %param.16) | copy-start | bytes 3145732
  5.8 1.2 %copy-start.3 = (f32[1,512,512]{2,1,0:T(8,128)S(1)}, f32[1,512,512]{2,1,0:T(8,128)}, u32[]{:S(2)}) copy-start(f32[1,512,512]{2,1,0:T(8,128)} %param.18) | copy-start | bytes 3145732
  7.0 0.9 %copy-start.4 = (f32[1,512,128]{2,1,0:T(8,128)S(1)}, f32[1,512,128]{2,1,0:T(8,128)}, u32[]{:S(2)}) copy-start(f32[1,512,128]{2,1,0:T(8,128)} %param.19) | copy-start | bytes 786436
  8.0 0.8 %copy-start.5 = (f32[128,128]{1,0:T(8,128)S(1)}, f32[128,128]{1,0:T(8,128)}, u32[]{:S(2)}) copy-start(f32[128,128]{1,0:T(8,128)} %cinv_hbm.1) | copy-start | bytes 196612
  8.8 0.8 %copy-start.6 = (f32[1,1,64,128]{3,2,1,0:T(8,128)S(1)}, f32[1,1,64,128]{3,2,1,0:T(8,128)}, u32[]{:S(2)}) copy-start(f32[1,1,64,128]{3,2,1,0:T(8,128)} %param.14) | copy-start | bytes 98308
  9.6 0.7 %copy-start.7 = (f32[1,1,32,64]{3,2,1,0:T(8,128)S(1)}, f32[1,1,32,64]{3,2,1,0:T(8,128)}, u32[]{:S(2)}) copy-start(f32[1,1,32,64]{3,2,1,0:T(8,128)} %param.17) | copy-start | bytes 24580
  10.3 0.7 %copy-start.8 = (s32[1,8]{1,0:T(1,128)S(1)}, s32[1,8]{1,0:T(1,128)}, u32[]{:S(2)}) copy-start(s32[1,8]{1,0:T(1,128)} %owners.1) | copy-start | bytes 100

commit v2 on v1

--- a/solution.py
+++ b/solution.py
@@ -47,7 +47,9 @@
     couplings,
     ranks,
     owners,
-    interior_hbm,
+    solved,
+    back,
+    lifted,
     own_out,
     linv,
     rhs,
@@ -56,26 +58,24 @@
     inverse,
     coarse,
     cinv,
-    g_basis,
-    g_irhs,
+    basis_own,
+    irhs_own,
+    pre_out,
+    pre_in,
     sums,
-    coarse_out,
-    in_sums,
-    in_coarse,
+    a_out,
+    a_in,
     mid,
-    in_mid,
-    g_sums,
-    g_coarse,
-    bct,
+    mid_in,
+    share,
+    lift_all,
+    sol,
+    own_stage,
+    own_in,
     gain,
     base,
-    solved,
-    back,
-    lifted,
-    result,
     leaf_sem,
     misc_sem,
-    out_sem,
     pre_send,
     pre_recv,
     a_send,
@@ -84,13 +84,15 @@
     m_recv,
     b_send,
     b_recv,
+    o_send,
+    o_recv,
 ):
     leaves, ls, ports = rhs.shape
-    blocks = couplings.shape[1]
-    rank = g_basis.shape[1]
-    cs = g_basis.shape[2]
-    nco = coarse.shape[2]
-    piece = nco // n
+    blocks = couplings.shape[2]
+    rank, cs = basis_own.shape
+    nco = coarse.shape[1]
+    part = ports // n
+    half_rank, half_part = rank // 2, part // 2
     me = lax.axis_index("sub")
     my_group = lax.axis_index("grp")
 
@@ -107,8 +109,8 @@
         for which in range(3):
             leaf_copy(l, which).start()
     misc = (
-        pltpu.make_async_copy(basis_hbm, g_basis.at[me], misc_sem.at[0]),
-        pltpu.make_async_copy(irhs_hbm, g_irhs.at[me], misc_sem.at[1]),
+        pltpu.make_async_copy(basis_hbm, basis_own, misc_sem.at[0]),
+        pltpu.make_async_copy(irhs_hbm, irhs_own, misc_sem.at[1]),
         pltpu.make_async_copy(coarse_hbm, coarse, misc_sem.at[2]),
         pltpu.make_async_copy(inverse_hbm, inverse, misc_sem.at[3]),
         pltpu.make_async_copy(cinv_hbm, cinv, misc_sem.at[4]),
@@ -127,13 +129,18 @@
         both = product(split(proj[l]), split(linv[l]))
         coef = narrow(split(both), split(rhs[l]))
         for j in range(blocks):
-            kept = jnp.where(row_of < ranks[l, j], coef[j * rank : (j + 1) * rank], 0.0)
+            kept = jnp.where(row_of < ranks[0, 0, j, l], coef[j * rank : (j + 1) * rank], 0.0)
             for k in range(n):
-                sums[k] += jnp.where(couplings[l, j] == k, kept, 0.0)
-
-    leaf_forward(0)
-
-    pl.semaphore_wait(barrier, n - 1 + groups - 1)
+                sums[k] += jnp.where(couplings[0, 0, j, l] == k, kept, 0.0)
+
+    misc[0].wait()
+    misc[1].wait()
+    packed = jnp.concatenate([basis_own[:half_rank], basis_own[half_rank:]], axis=1)
+    irhs_t = irhs_own[...].T
+    for t in range(n):
+        pre_out[t, :half_rank] = packed
+        rows = irhs_t[t * part : (t + 1) * part]
+        pre_out[t, half_rank:] = jnp.concatenate([rows[:half_part], rows[half_part:]], axis=1)
 
     def peer(d):
         return (lax.rem(me + d, n), my_group)
@@ -141,94 +148,72 @@
     def source(d):
         return lax.rem(me - d + n, n)
 
-    def pre_copy(d, which, slot):
-        src, dst = ((basis_hbm, g_basis), (irhs_hbm, g_irhs))[which]
+    def remote(src, dst, send, recv, target):
         return pltpu.make_async_remote_copy(
-            src_ref=src, dst_ref=dst.at[slot], send_sem=pre_send.at[which, d], recv_sem=pre_recv.at[which, d],
-            device_id=peer(d), device_id_type=MESH,
+            src_ref=src, dst_ref=dst, send_sem=send, recv_sem=recv, device_id=target, device_id_type=MESH
         )
 
-    for which in range(2):
-        for d in range(1, n):
-            pre_copy(d, which, me).start()
-
-    pl.loop(1, leaves)(leaf_forward)
+    def pre_copy(d, slot):
+        return remote(pre_out.at[lax.rem(me + d, n)], pre_in.at[slot], pre_send.at[d], pre_recv.at[d], peer(d))
 
     def sums_copy(d):
-        return pltpu.make_async_remote_copy(
-            src_ref=sums.at[lax.rem(me + d, n)], dst_ref=in_sums.at[d], send_sem=a_send.at[0, d],
-            recv_sem=a_recv.at[0, d], device_id=peer(d), device_id_type=MESH,
-        )
-
-    def coarse_copy(d):
-        return pltpu.make_async_remote_copy(
-            src_ref=coarse_out.at[lax.rem(me + d, n)], dst_ref=in_coarse.at[d], send_sem=a_send.at[1, d],
-            recv_sem=a_recv.at[1, d], device_id=peer(d), device_id_type=MESH,
-        )
-
+        return remote(a_out.at[lax.rem(me + d, n)], a_in.at[d], a_send.at[d], a_recv.at[d], peer(d))
+
+    def mid_copy(d):
+        target = (me, lax.rem(my_group + d, groups))
+        return remote(mid, mid_in.at[d], m_send.at[d], m_recv.at[d], target)
+
+    def gather_copy(d, slot):
+        return remote(share, lift_all.at[slot], b_send.at[d], b_recv.at[d], peer(d))
+
+    def own_copy(d, slot):
+        return remote(own_stage.at[lax.rem(me + d, n)], own_in.at[slot], o_send.at[d], o_recv.at[d], peer(d))
+
+    pl.semaphore_wait(barrier, n - 1 + groups - 1)
+    for d in range(1, n):
+        pre_copy(d, me).start()
+    pre_in[me] = pre_out[me]
+
+    pl.loop(0, leaves)(leaf_forward)
+
+    sums_t = sums[...].reshape(n * rank, ports).T
+    a_out[...] = sums_t.reshape(n, part, n * rank)
     for d in range(1, n):
         sums_copy(d).start()
 
-    for copy in misc:
+    for copy in misc[2:]:
         copy.wait()
-    for which in range(2):
-        for d in range(1, n):
-            pre_copy(d, which, source(d)).wait_recv()
-
-    stacked = jnp.concatenate([g_basis[owners[0, k]] for k in range(n)], axis=0)
+    for d in range(1, n):
+        pre_copy(d, source(d)).wait_recv()
+    got = [pre_in[owners[0, k]] for k in range(n)]
+    stacked = jnp.concatenate(
+        [half for g in got for half in (g[:half_rank, :cs], g[:half_rank, cs:])], axis=0
+    )
     wide = jnp.concatenate([stacked] * n, axis=1)
     diag_row = lax.broadcasted_iota(jnp.int32, wide.shape, 0) // rank
     diag_col = lax.broadcasted_iota(jnp.int32, wide.shape, 1) // cs
     diagonal = split(jnp.where(diag_row == diag_col, wide, 0.0))
-    own = jnp.int32(0)
-    for k in range(n):
-        own = jnp.where(owners[0, k] == me, k, own)
-    coarse_pair = split(coarse[...].reshape(n * cs, nco))
+    irhs_share = jnp.concatenate(
+        [jnp.concatenate([g[half_rank:, :cs], g[half_rank:, cs:]], axis=0) for g in got], axis=1
+    )
+    irhs_pair = split(irhs_share)
+    coarse_pair = split(coarse[...])
+    inverse_pair = split(inverse[...])
     basis_coarse = narrow(diagonal, coarse_pair)
-    own_coarse = coarse[own]
-    bct[...] = basis_coarse.T
-    sums_pair = split(sums[...].reshape(n * rank, ports))
-    part = narrow(split(own_coarse.T), split(g_irhs[me])) - narrow(split(bct[...]), sums_pair)
-    coarse_out[...] = part.reshape(n, piece, ports)
-    for d in range(1, n):
-        coarse_copy(d).start()
-
-    own_rows = inverse[own]
-    inverse_pair = split(inverse[...].reshape(n * cs, n * cs))
-    left = jnp.concatenate([product(diagonal, inverse_pair), own_rows], axis=0)
-    left_pair = split(left)
-    irhs_all = jnp.concatenate([g_irhs[owners[0, k]] for k in range(n)], axis=0)
-    base[...] = narrow(left_pair, split(irhs_all))
+    basis_coarse_pair = split(basis_coarse)
+    left_pair = split(product(diagonal, inverse_pair))
+    base[...] = product(irhs_pair, left_pair, ((1,), (1,)))
     gain[:, : n * rank] = -product(left_pair, diagonal, ((1,), (1,)))
-    coarse_left = jnp.concatenate([basis_coarse, own_coarse], axis=0)
-    gain[:, n * rank :] = narrow(split(coarse_left), split(cinv[...]))
-
-    def gather_copy(d, which, slot):
-        ref = (g_sums, g_coarse)[which]
-        return pltpu.make_async_remote_copy(
-            src_ref=ref.at[me], dst_ref=ref.at[slot], send_sem=b_send.at[which, d], recv_sem=b_recv.at[which, d],
-            device_id=peer(d), device_id_type=MESH,
-        )
-
-    total = sums[me]
+    gain[:, n * rank :] = narrow(basis_coarse_pair, split(cinv[...]))
+    coarse_base = narrow(irhs_pair, coarse_pair)
+
+    total = a_out[me]
     for d in range(1, n):
         sums_copy(d).wait_recv()
-        total = total + in_sums[d]
-    g_sums[me] = total
-    for d in range(1, n):
-        gather_copy(d, 0, me).start()
-
-    def mid_copy(d):
-        return pltpu.make_async_remote_copy(
-            src_ref=mid, dst_ref=in_mid.at[d], send_sem=m_send.at[d], recv_sem=m_recv.at[d],
-            device_id=(me, lax.rem(my_group + d, groups)), device_id_type=MESH,
-        )
-
-    coarse_total = coarse_out[me]
-    for d in range(1, n):
-        coarse_copy(d).wait_recv()
-        coarse_total = coarse_total + in_coarse[d]
-    mid[...] = coarse_total
+        total = total + a_in[d]
+    total_pair = split(total)
+    residual = coarse_base - narrow(total_pair, basis_coarse_pair)
+    mid[...] = residual
     for d in range(1, groups):
         mid_copy(d).start()
 
@@ -244,45 +229,71 @@
 
     for d in range(1, groups):
         mid_copy(d).wait_recv()
-        coarse_total = coarse_total + in_mid[d]
-    g_coarse[me] = coarse_total
-    for d in range(1, n):
-        gather_copy(d, 1, me).start()
+        residual = residual + mid_in[d]
+    known = jnp.concatenate([total, residual], axis=1)
+    share[...] = base[...] + product(split(known), split(gain[...]), ((1,), (1,)))
+    for d in range(1, n):
+        gather_copy(d, me).start()
+    lift_all[me] = share[...]
+
+    by_cluster = split(irhs_share - product(total_pair, diagonal))
+    coarse_solution = split(product(split(residual), split(cinv[...]), ((1,), (1,))))
+    solution_t = product(by_cluster, inverse_pair, ((1,), (1,))) + product(coarse_solution, coarse_pair, ((1,), (1,)))
+    for k in range(n):
+        rows = solution_t[:, k * cs : (k + 1) * cs]
+        sol[k] = jnp.concatenate([rows[:half_part], rows[half_part:]], axis=1)
+    for t in range(n):
+        place = jnp.int32(0)
+        for k in range(n):
+            place = jnp.where(owners[0, k] == t, k, place)
+        own_stage[t] = sol[place]
+    for d in range(1, n):
+        own_copy(d, me).start()
+    own_in[me] = own_stage[me]
 
     pl.loop(half, leaves)(leaf_middle)
 
-    for which in range(2):
-        for d in range(1, n):
-            gather_copy(d, which, source(d)).wait_recv()
-
-    known = jnp.concatenate([g_sums[...].reshape(n * rank, ports), g_coarse[...].reshape(nco, ports)], axis=0)
-    final = base[...] + narrow(split(gain[...]), split(known))
-    lifted[...] = final[: n * rank].reshape(n, rank, ports)
-    own_out[...] = final[n * rank :]
+    for d in range(1, n):
+        gather_copy(d, source(d)).wait_recv()
+    lifted[...] = lift_all[...].reshape(ports, n * rank).T.reshape(n, rank, ports)
+    for d in range(1, n):
+        own_copy(d, source(d)).wait_recv()
+    rows = []
+    for t in range(n):
+        rows += [own_in[t][:, :cs], own_in[t][:, cs:]]
+    own_out[...] = jnp.concatenate(rows, axis=0).T
+
+    for d in range(1, n):
+        pre_copy(d, me).wait_send()
+        sums_copy(d).wait_send()
+        gather_copy(d, me).wait_send()
+        own_copy(d, me).wait_send()
+    for d in range(1, groups):
+        mid_copy(d).wait_send()
+
+
+def finish(solved, back, lifted, own, couplings, ranks, interior_hbm, own_hbm, result, out_sem, own_sem):
+    leaves, ls, ports = solved.shape
+    blocks = couplings.shape[2]
+    rank = lifted.shape[1]
+    row_of = lax.broadcasted_iota(jnp.int32, (rank, ports), 0)
+    own_copy = pltpu.make_async_copy(own, own_hbm, own_sem)
+    own_copy.start()
 
     def out_copy(l):
         return pltpu.make_async_copy(result.at[l], interior_hbm.at[l], out_sem.at[l])
 
-    @pl.loop(0, leaves)
-    def leaf_back(l):
+    for l in range(leaves):
         rows = []
         for j in range(blocks):
-            rows.append(jnp.where(row_of < ranks[l, j], lifted[couplings[l, j]], 0.0))
+            rows.append(jnp.where(row_of < ranks[0, 0, j, l], lifted[couplings[0, 0, j, l]], 0.0))
         pair = jnp.concatenate(split(jnp.concatenate(rows, axis=0)), axis=1)
         both = dot(back[l], jnp.concatenate([pair, pair], axis=0))
         result[l] = solved[l] - (both[:, :ports] + both[:, ports:])
         out_copy(l).start()
-
     for l in range(leaves):
         out_copy(l).wait()
-    for d in range(1, n):
-        for which in range(2):
-            pre_copy(d, which, me).wait_send()
-            gather_copy(d, which, me).wait_send()
-        sums_copy(d).wait_send()
-        coarse_copy(d).wait_send()
-    for d in range(1, groups):
-        mid_copy(d).wait_send()
+    own_copy.wait()
 
 
 def fused(
@@ -307,57 +318,55 @@
     cs = cluster_basis.shape[3]
     nig = interface_inverse.shape[1]
     nco = coarse_basis.shape[2]
-    piece = nco // n
-    hbm = pl.BlockSpec(memory_space=pl.ANY)
+    part = ports // n
+    hbm = pl.BlockSpec(memory_space=pltpu.HBM)
     smem = pl.BlockSpec(memory_space=pltpu.SMEM)
+    vmem = pl.BlockSpec(memory_space=pltpu.VMEM)
     dma = pltpu.SemaphoreType.DMA
-    interior, own = pl.pallas_call(
+    couplings = jnp.swapaxes(couplings, 2, 3)
+    ranks = jnp.swapaxes(ranks, 2, 3)
+    held = pl.pallas_call(
         functools.partial(kernel, n, groups),
         out_shape=(
-            jax.ShapeDtypeStruct((leaves, ls, ports), F32),
-            jax.ShapeDtypeStruct((cs, ports), F32),
+            pltpu.VMEM((leaves, ls, ports), F32),
+            pltpu.VMEM((leaves, ls, 2 * blocks * rank), BF16),
+            pltpu.VMEM((n, rank, ports), F32),
+            pltpu.VMEM((cs, ports), F32),
         ),
         in_specs=[hbm] * 9 + [smem] * 3,
-        out_specs=(hbm, pl.BlockSpec(memory_space=pltpu.VMEM)),
+        out_specs=(vmem,) * 4,
         scratch_shapes=[
             pltpu.VMEM((leaves, ls, ls), F32),
             pltpu.VMEM((leaves, ls, ports), F32),
             pltpu.VMEM((leaves, blocks * rank, ls), F32),
             pltpu.VMEM((leaves, blocks * rank, ls), F32),
-            pltpu.VMEM((n, cs, nig), F32),
-            pltpu.VMEM((n, cs, nco), F32),
+            pltpu.VMEM((nig, nig), F32),
+            pltpu.VMEM((nig, nco), F32),
             pltpu.VMEM((nco, nco), F32),
-            pltpu.VMEM((n, rank, cs), F32),
-            pltpu.VMEM((n, cs, ports), F32),
+            pltpu.VMEM((rank, cs), F32),
+            pltpu.VMEM((cs, ports), F32),
+            pltpu.VMEM((n, rank // 2 + part // 2, 2 * cs), F32),
+            pltpu.VMEM((n, rank // 2 + part // 2, 2 * cs), F32),
             pltpu.VMEM((n, rank, ports), F32),
-            pltpu.VMEM((n, piece, ports), F32),
-            pltpu.VMEM((n, rank, ports), F32),
-            pltpu.VMEM((n, piece, ports), F32),
-            pltpu.VMEM((piece, ports), F32),
-            pltpu.VMEM((groups, piece, ports), F32),
-            pltpu.VMEM((n, rank, ports), F32),
-            pltpu.VMEM((n, piece, ports), F32),
-            pltpu.VMEM((nco, n * rank), F32),
-            pltpu.VMEM((n * rank + cs, n * rank + nco), F32),
-            pltpu.VMEM((n * rank + cs, ports), F32),
-            pltpu.VMEM((leaves, ls, ports), F32),
-            pltpu.VMEM((leaves, ls, 2 * blocks * rank), BF16),
-            pltpu.VMEM((n, rank, ports), F32),
-            pltpu.VMEM((leaves, ls, ports), F32),
+            pltpu.VMEM((n, part, n * rank), F32),
+            pltpu.VMEM((n, part, n * rank), F32),
+            pltpu.VMEM((part, nco), F32),
+            pltpu.VMEM((groups, part, nco), F32),
+            pltpu.VMEM((part, n * rank), F32),
+            pltpu.VMEM((n, part, n * rank), F32),
+            pltpu.VMEM((n, part // 2, 2 * cs), F32),
+            pltpu.VMEM((n, part // 2, 2 * cs), F32),
+            pltpu.VMEM((n, part // 2, 2 * cs), F32),
+            pltpu.VMEM((n * rank, n * rank + nco), F32),
+            pltpu.VMEM((part, n * rank), F32),
             dma((4, leaves)),
             dma((5,)),
-            dma((leaves,)),
-            dma((2, n)),
-            dma((2, n)),
-            dma((2, n)),
-            dma((2, n)),
-            dma((groups,)),
-            dma((groups,)),
-            dma((2, n)),
-            dma((2, n)),
-        ],
+        ]
+        + [dma((n,))] * 4
+        + [dma((groups,))] * 2
+        + [dma((n,))] * 4,
         compiler_params=pltpu.CompilerParams(
-            collective_id=0, has_side_effects=True, vmem_limit_bytes=48 * 1024 * 1024
+            collective_id=0, has_side_effects=True, vmem_limit_bytes=61 * 1024 * 1024
         ),
     )(
         leaf_inverse[0, 0],
@@ -366,13 +375,24 @@
         project_basis.reshape(leaves, blocks * rank, ls),
         lift_basis.reshape(leaves, blocks * rank, ls),
         cluster_basis[0, 0],
-        interface_inverse.reshape(n, cs, nig),
-        coarse_basis.reshape(n, cs, nco),
+        interface_inverse[0],
+        coarse_basis[0],
         coarse_inverse,
-        couplings[0, 0],
-        ranks[0, 0],
+        couplings,
+        ranks,
         owners,
     )
+    interior, own = pl.pallas_call(
+        finish,
+        out_shape=(
+            jax.ShapeDtypeStruct((leaves, ls, ports), F32),
+            jax.ShapeDtypeStruct((cs, ports), F32),
+        ),
+        in_specs=[vmem] * 4 + [smem] * 2,
+        out_specs=(hbm, hbm),
+        scratch_shapes=[pltpu.VMEM((leaves, ls, ports), F32), dma((leaves,)), dma],
+        compiler_params=pltpu.CompilerParams(vmem_limit_bytes=16 * 1024 * 1024),
+    )(*held, couplings, ranks)
     return interior[None, None], own[None, None]
 
 

time: 50.6 us -> 29 us (0.57)
  local copies, waits for them, and re-layouts: 11.9 us -> 0.01 us
  Pallas kernels: 37.5 us -> 28.1 us
    unnamed x20 -> x4, local copies, waits for them, and re-layouts: 10.4 us -> 0.01 us
    pallas_call x1 -> x2, Pallas kernels: 37.5 us -> 28.1 us  [the longest x1 26.2 us: fused(): pl.pallas_call(functools.partial(kernel, n, groups), out_shape=(pltpu.VME...]
    squeeze x2 -> x0, local copies, waits for them, and re-layouts: 1.51 us -> none  [the longest x1 0.76 us: fused(): couplings[0, 0]]
where the time goes in v2:
time: 29 us; the launch traced here: 28.8 us
  Pallas kernels  28.1 us (97%)
  between operations  0.67 us (2%)
    pallas_call x1, Pallas kernels, fused(): pl.pallas_call(functools.partial(kernel, n, groups), out_shape=(pltpu.VME...  26.2 us
    pallas_call x1, Pallas kernels, fused(): pl.pallas_call(finish, out_shape=(jax.ShapeDtypeStruct((leaves, ls, ports...  1.91 us

profile of v2, /device:TPU:0, one launch (start us, length us, event | category | flops | bytes accessed | tf_op | source)
XLA Modules:
  0.0 28.8 jit_solution(8794326233938554885)
XLA Ops:
  0.6 0.0 copy-start
  0.6 0.0 copy-start.1
  0.7 26.2 %shard_map.131 = (f32[8,256,128]{2,1,0:T(8,128)S(1)}, bf16[8,256,256]{2,1,0:T(8,128)(2,1)S(1)}, f32[8,32,128]{2,1,0:T(8,128)S(1)}, f32[64,128]{1,0:T(8,128)S(1)}) custom-call(f32[8,256,256]{2,1,0:T(8,128)} %bitcast.16, f32[8,256,128]{2,1,0:T(8,128)} %bitcast.17, f32[64,128]{1,0:T(8,128)} %bitcast.22, f32[8,128,256]{2,1,0:T(8,128)} %bitcast.18, ...), custom_call_target="tpu_custom_call" | custom-call | tf_op jit(solution)/shard_map/pallas_call | solution.py:328
  26.9 0.0 copy-done
  26.9 0.0 copy-done.1
  26.9 1.9 %shard_map.132 = (f32[8,256,128]{2,1,0:T(8,128)}, f32[64,128]{1,0:T(8,128)}) custom-call(f32[8,256,128]{2,1,0:T(8,128)S(1)} %get-tuple-element.8.solved, bf16[8,256,256]{2,1,0:T(8,128)(2,1)S(1)} %get-tuple-element.9.back, f32[8,32,128]{2,1,0:T(8,128)S(1)} %get-tuple-element.10.lifted, f32[64,128]{1,0:T(8,128)S(1)} %get-tuple-element.11.own, ...), custom_call_target="tpu_custom_call" | custom-call | tf_op jit(solution)/shard_map/pallas_call | solution.py:385
Async XLA Ops:
  0.6 26.2 %copy-start = (s32[1,1,8,4]{2,3,1,0:T(4,128)S(1)}, s32[1,1,8,4]{2,3,1,0:T(4,128)}, u32[]{:S(2)}) copy-start(s32[1,1,8,4]{2,3,1,0:T(4,128)} %param.21) | copy-start | bytes 388
  0.6 26.2 %copy-start.1 = (s32[1,1,8,4]{2,3,1,0:T(4,128)S(1)}, s32[1,1,8,4]{2,3,1,0:T(4,128)}, u32[]{:S(2)}) copy-start(s32[1,1,8,4]{2,3,1,0:T(4,128)} %param.22) | copy-start | bytes 388

commit v3 on v2

--- a/solution.py
+++ b/solution.py
@@ -169,12 +169,15 @@
     def own_copy(d, slot):
         return remote(own_stage.at[lax.rem(me + d, n)], own_in.at[slot], o_send.at[d], o_recv.at[d], peer(d))
 
+    early = leaves * 2 // 8
+    pl.loop(0, early)(leaf_forward)
+
     pl.semaphore_wait(barrier, n - 1 + groups - 1)
     for d in range(1, n):
         pre_copy(d, me).start()
     pre_in[me] = pre_out[me]
 
-    pl.loop(0, leaves)(leaf_forward)
+    pl.loop(early, leaves)(leaf_forward)
 
     sums_t = sums[...].reshape(n * rank, ports).T
     a_out[...] = sums_t.reshape(n, part, n * rank)

time: 29 us -> 28.3 us (0.976)
  Pallas kernels: 28.1 us -> 27.5 us
    pallas_call x1, Pallas kernels: 26.2 us -> 25.6 us  [fused(): pl.pallas_call(functools.partial(kernel, n, groups), out_shape=(pltpu.VME...]
where the time goes in v3:
time: 28.3 us; the launch traced here: 28.2 us
  Pallas kernels  27.5 us (97%)
  between operations  0.67 us (2%)
    pallas_call x1, Pallas kernels, fused(): pl.pallas_call(functools.partial(kernel, n, groups), out_shape=(pltpu.VME...  25.6 us
    pallas_call x1, Pallas kernels, fused(): pl.pallas_call(finish, out_shape=(jax.ShapeDtypeStruct((leaves, ls, ports...  1.91 us

profile of v3, /device:TPU:0, one launch (start us, length us, event | category | flops | bytes accessed | tf_op | source)
XLA Modules:
  0.0 28.2 jit_solution(3950605001150206022)
XLA Ops:
  0.6 0.0 copy-start
  0.6 0.0 copy-start.1
  0.7 25.6 %shard_map.131 = (f32[8,256,128]{2,1,0:T(8,128)S(1)}, bf16[8,256,256]{2,1,0:T(8,128)(2,1)S(1)}, f32[8,32,128]{2,1,0:T(8,128)S(1)}, f32[64,128]{1,0:T(8,128)S(1)}) custom-call(f32[8,256,256]{2,1,0:T(8,128)} %bitcast.16, f32[8,256,128]{2,1,0:T(8,128)} %bitcast.17, f32[64,128]{1,0:T(8,128)} %bitcast.22, f32[8,128,256]{2,1,0:T(8,128)} %bitcast.18, ...), custom_call_target="tpu_custom_call" | custom-call | tf_op jit(solution)/shard_map/pallas_call | solution.py:331
  26.2 0.0 copy-done
  26.2 0.0 copy-done.1
  26.2 1.9 %shard_map.132 = (f32[8,256,128]{2,1,0:T(8,128)}, f32[64,128]{1,0:T(8,128)}) custom-call(f32[8,256,128]{2,1,0:T(8,128)S(1)} %get-tuple-element.8.solved, bf16[8,256,256]{2,1,0:T(8,128)(2,1)S(1)} %get-tuple-element.9.back, f32[8,32,128]{2,1,0:T(8,128)S(1)} %get-tuple-element.10.lifted, f32[64,128]{1,0:T(8,128)S(1)} %get-tuple-element.11.own, ...), custom_call_target="tpu_custom_call" | custom-call | tf_op jit(solution)/shard_map/pallas_call | solution.py:388
Async XLA Ops:
  0.6 25.6 %copy-start = (s32[1,1,8,4]{2,3,1,0:T(4,128)S(1)}, s32[1,1,8,4]{2,3,1,0:T(4,128)}, u32[]{:S(2)}) copy-start(s32[1,1,8,4]{2,3,1,0:T(4,128)} %param.21) | copy-start | bytes 388
  0.6 25.6 %copy-start.1 = (s32[1,1,8,4]{2,3,1,0:T(4,128)S(1)}, s32[1,1,8,4]{2,3,1,0:T(4,128)}, u32[]{:S(2)}) copy-start(s32[1,1,8,4]{2,3,1,0:T(4,128)} %param.22) | copy-start | bytes 388
